TPU v7x, 32 devices: a whole 2x2x4 slice. The times are simulated.
32 devices in a mesh: groups: 2 (over y), row: 4 (over z), col: 2 (over x), sub: 2 (over core).
Axes of the slice: x: 2, y: 2, z: 4, core: 2. Of those that a mesh axis runs over, the one named last changes fastest.
Arguments:
- densities: float32 [2, 4, 32768], P(None, None, ('groups', 'row', 'col', 'sub')), parts along dimension 2, may hold values from -6 to 6
- positions: float32 [3, 32768], P(None, ('groups', 'row', 'col', 'sub')), parts along dimension 1, may hold values from -5 to 5
- normals: float32 [3, 32768], P(None, ('groups', 'row', 'col', 'sub')), parts along dimension 1, may hold values from -3 to 3
- weights: float32 [32768], P(('groups', 'row', 'col', 'sub')), parts along dimension 0, may hold values from 0.3 to 1
- cluster_panels: int32 [32, 1024], P(('groups', 'row', 'col', 'sub')), parts along dimension 0, may hold values from 0 to 1023, each once within a row
- pair_list: int32 [2, 384], P(None, ('groups', 'row', 'col', 'sub')), parts along dimension 1, may hold values from 0 to 31, as said below
- quad_order: int32 [384], P(('groups', 'row', 'col', 'sub')), parts along dimension 0, may hold values from 1 to 4
- pair_count: int32 [32], P(('groups', 'row', 'col', 'sub')), parts along dimension 0, may hold values from 3 to 12, as said below
Outputs:
- layer_potentials: float32 [2, 4, 32768], P(None, None, ('groups', 'row', 'col', 'sub')), parts along dimension 2
There are 2 independent parts, one for each index of `groups`. A program takes and returns all parts, laid end to end along the dimension named above; each array names one. Nothing has to cross between parts.
Inputs may be any that keep to these rules, and one draw needn't show every extreme that they name: `pair_list`: row 0 lies below 16 and row 1 below 32; every slot, used or not, holds a valid pair; no unordered pair of clusters stands in two slots of a problem, and a cluster may be paired with itself. `pair_count`: the used slots of a device are its first ones; the two devices of one grid cell hold 15 used slots together, and some device holds exactly 12.
All inputs are finite; a program needn't handle non-finite values.
Results may differ from a plain program's by a relative error of at most 0.0003.
Values sent between devices are 32-bit elements; how exact they have to be, the bound alone decides.
A program may use at most 128 MiB of HBM per device.

v0:
```python
from functools import partial

import jax
import jax.numpy as jnp
from jax import lax
from jax.sharding import PartitionSpec as P

PANEL = 256


wavenumber = 3.0
soften = 0.5
four_pi = 12.566370614359172


def kernels(row_geom, col_geom, quad_level):
    offset = row_geom[0:3, :, None] - col_geom[0:3, None, :]
    soften_sq = (soften / quad_level.astype(jnp.float32)) ** 2
    rho_sq = jnp.sum(offset * offset, axis=0) + soften_sq
    distance = jnp.sqrt(rho_sq)
    phase_arg = wavenumber * distance
    cosine = jnp.cos(phase_arg)
    single = cosine / (four_pi * distance)
    radial = (cosine + phase_arg * jnp.sin(phase_arg)) / (four_pi * rho_sq * distance)
    row_weight = row_geom[6][:, None]
    col_weight = col_geom[6][None, :]
    along_col = jnp.sum(offset * col_geom[3:6, None, :], axis=0)
    along_row = jnp.sum(offset * row_geom[3:6, :, None], axis=0)
    return (
        row_weight * col_weight * single,
        row_weight * radial * along_col,
        -col_weight * radial * along_row,
    )


def apply_rows(tile, dens):
    return jnp.einsum("ij,rj->ri", tile, dens, precision=lax.Precision.HIGHEST)


def apply_cols(tile, dens):
    return jnp.einsum("ij,ri->rj", tile, dens, precision=lax.Precision.HIGHEST)


def contributions(row_geom, col_geom, quad_level, nrhs):
    single, double, adjoint = kernels(row_geom, col_geom, quad_level)
    row_sigma = row_geom[7 : 7 + nrhs]
    row_mu = row_geom[7 + nrhs :]
    col_sigma = col_geom[7 : 7 + nrhs]
    col_mu = col_geom[7 + nrhs :]
    onto_row = jnp.stack(
        [apply_rows(single, col_sigma) + apply_rows(double, col_mu), apply_rows(adjoint, col_sigma)]
    )
    onto_col = jnp.stack(
        [apply_cols(single, row_sigma) + apply_cols(adjoint, row_mu), apply_cols(double, row_sigma)]
    )
    return (onto_row, onto_col)


def body(densities, positions, normals, weights, cluster_panels, pair_list, quad_order, pair_count):
    rhs_count = densities.shape[1]
    own_panels = positions.shape[1]
    stacked = jnp.concatenate(
        [positions, normals, weights[None, :], densities.reshape(2 * rhs_count, own_panels)], axis=0
    )
    ordered = jnp.take(stacked, cluster_panels[0], axis=1)
    row_data = lax.all_gather(ordered, ("col", "sub"), axis=1, tiled=True)
    col_data = lax.all_gather(ordered, ("row", "sub"), axis=1, tiled=True)
    slots_dev = pair_list.shape[1]
    row_local = pair_list[0]
    col_local = pair_list[1]
    used_slots = pair_count[0]
    col_size = lax.axis_size("col")
    sub_size = lax.axis_size("sub")
    clusters_dev = own_panels // PANEL
    row_cluster = lax.axis_index("row") * (clusters_dev * col_size * sub_size) + row_local
    col_cluster = (
        (col_local // (sub_size * clusters_dev) * col_size + lax.axis_index("col")) * sub_size
        + col_local // clusters_dev % sub_size
    ) * clusters_dev + col_local % clusters_dev
    per_turn = 2
    turn_count = (used_slots + per_turn - 1) // per_turn
    pair_terms = jax.vmap(partial(contributions, nrhs=rhs_count))

    def one_turn(turn_index, sums):
        row_sums, col_sums = sums
        slot_ids = turn_index * per_turn + jnp.arange(per_turn, dtype=jnp.int32)
        in_use = slot_ids < used_slots
        safe_ids = jnp.minimum(slot_ids, slots_dev - 1)
        row_pick = row_local[safe_ids]
        col_pick = col_local[safe_ids]
        not_self = row_cluster[safe_ids] != col_cluster[safe_ids]
        row_geoms = jax.vmap(lambda spot_at: lax.dynamic_slice_in_dim(row_data, spot_at, PANEL, 1))(
            row_pick * PANEL
        )
        col_geoms = jax.vmap(lambda spot_at: lax.dynamic_slice_in_dim(col_data, spot_at, PANEL, 1))(
            col_pick * PANEL
        )
        onto_row, onto_col = pair_terms(row_geoms, col_geoms, quad_order[safe_ids])
        onto_row = jnp.where(in_use[:, None, None, None], onto_row, 0.0)
        onto_col = jnp.where((in_use & not_self)[:, None, None, None], onto_col, 0.0)
        for member in range(per_turn):
            row_start = row_pick[member] * PANEL
            current = lax.dynamic_slice_in_dim(row_sums, row_start, PANEL, 2)
            row_sums = lax.dynamic_update_slice_in_dim(
                row_sums, current + onto_row[member], row_start, 2
            )
            col_start = col_pick[member] * PANEL
            current = lax.dynamic_slice_in_dim(col_sums, col_start, PANEL, 2)
            col_sums = lax.dynamic_update_slice_in_dim(
                col_sums, current + onto_col[member], col_start, 2
            )
        return (row_sums, col_sums)

    start_sums = (
        jnp.zeros((2, rhs_count, row_data.shape[1]), jnp.float32),
        jnp.zeros((2, rhs_count, col_data.shape[1]), jnp.float32),
    )
    row_sums, col_sums = lax.fori_loop(0, turn_count, one_turn, start_sums)
    combined = lax.psum_scatter(
        row_sums, ("col", "sub"), scatter_dimension=2, tiled=True
    ) + lax.psum_scatter(col_sums, ("row", "sub"), scatter_dimension=2, tiled=True)
    return jnp.zeros_like(combined).at[:, :, cluster_panels[0]].set(combined)


def solution(mesh):
    placed = (
        P(None, None, ("groups", "row", "col", "sub")),
        P(None, ("groups", "row", "col", "sub")),
        P(None, ("groups", "row", "col", "sub")),
        P(("groups", "row", "col", "sub")),
        P(("groups", "row", "col", "sub"), None),
        P(None, ("groups", "row", "col", "sub")),
        P(("groups", "row", "col", "sub")),
        P(("groups", "row", "col", "sub")),
    )
    return jax.shard_map(
        body,
        mesh=mesh,
        in_specs=placed,
        out_specs=P(None, None, ("groups", "row", "col", "sub")),
        check_vma=False,
    )
```

profile of v0, /device:TPU:0, one launch (start us, length us, event | category | flops | bytes accessed | tf_op | source)
XLA Modules:
  0.0 346.7 jit_solution(15823528499711863039)
XLA Ops:
  7.2 0.7 compare_select_fusion.3
  7.9 0.8 reshape.123
  8.7 0.8 pad_maximum_fusion
  9.7 0.7 compare_and_fusion.1
  10.4 2.8 gather_fusion.5
  13.4 41.4 %all_gather.6 = f32[15,8192]{0,1:T(8,128)} all-gather(f32[15,1024]{0,1:T(8,128)S(1)} %select_bitcast_fusion), channel_id=1, replica_groups=mesh['groups'=2,'row'=4,'col'=2,'sub'=2] {'row','sub'}, dimensions={1}, use_global_device_ids=true | all-gather | bytes 552960 | tf_op jit(solution)/shard_map/all_gather | solution.py:67
  54.8 15.8 %all_gather.7 = f32[15,4096]{0,1:T(8,128)S(1)} all-gather(f32[15,1024]{0,1:T(8,128)S(1)} %select_bitcast_fusion), channel_id=1, replica_groups=mesh['groups'=2,'row'=4,'col'=2,'sub'=2] {'col','sub'}, dimensions={1}, use_global_device_ids=true | all-gather | bytes 307200 | tf_op jit(solution)/shard_map/all_gather | solution.py:66
  70.6 2.8 copy.46
  74.2 0.7 broadcast_in_dim.57
  74.9 0.7 broadcast_in_dim.56
  75.6 91.7 %while.18 = (s32[]{:T(128)}, f32[2,4,4096]{2,1,0:T(4,128)}, f32[2,4,8192]{2,1,0:T(4,128)}, s32[]{:T(128)}, s32[12]{0:T(128)S(1)}, /*index=5*/s32[]{:T(128)}, s32...) while((s32[]{:T(128)}, f32[2,4,4096]{2,1,0:T(4,128)}, ...), condition=%wide.region_4.5_spmd, body=%wide.region_0.4_spmd.sunk | while | flops 42628660 | bytes 8907799 | solution.py:118
  75.6 0.6 gather_fusion
  76.5 2.4 while.19
  78.9 0.6 gather_fusion.1
  79.7 2.4 while.20
  82.7 0.6 gather_fusion.2
  83.4 2.4 divide_multiply_fusion.5
  87.4 0.7 gather_fusion.3
  88.1 0.6 gather_fusion.4
  88.7 0.7 compare_and_fusion.3
  92.1 0.7 fusion.69
  93.3 1.3 fusion.81
  95.4 1.3 fusion.83
  97.2 1.3 fusion.82
  99.4 2.4 while.19
  102.6 2.4 while.20
  106.3 2.4 divide_multiply_fusion.5
  110.3 0.7 gather_fusion.3
  111.6 0.7 compare_and_fusion.3
  115.0 0.7 fusion.69
  116.3 1.4 fusion.81
  118.3 1.3 fusion.83
  120.2 1.3 fusion.82
  122.3 2.4 while.19
  125.6 2.4 while.20
  129.2 2.4 divide_multiply_fusion.5
  133.3 0.7 gather_fusion.3
  133.9 0.6 gather_fusion.4
  134.6 0.7 compare_and_fusion.3
  137.9 0.7 fusion.69
  139.2 1.3 fusion.81
  141.2 1.3 fusion.83
  143.1 1.3 fusion.82
  145.2 2.4 while.19
  148.5 2.4 while.20
  152.1 2.4 divide_multiply_fusion.5
  156.2 0.7 gather_fusion.3
  156.8 0.6 gather_fusion.4
  157.5 0.7 compare_and_fusion.3
  160.8 0.7 fusion.69
  162.1 1.3 fusion.81
  164.1 1.3 fusion.83
  166.0 1.3 fusion.82
  167.3 5.3 %copy.50 = f32[2,4,4096]{1,0,2:T(2,128)} copy(f32[2,4,4096]{2,1,0:T(4,128)} %get-tuple-element.69) | data formatting | bytes 262144
  172.6 5.4 %reshape.218 = f32[4096,8]{1,0:T(8,128)} reshape(f32[4096,2,4]{2,1,0:T(2,128)} %bitcast.141) | data formatting | bytes 262144
  178.2 0.7 copy-done.1
  178.9 7.8 %copy.52 = f32[2,4,8192]{1,0,2:T(2,128)} copy(f32[2,4,8192]{2,1,0:T(4,128)S(1)} %copy-done.1) | data formatting | bytes 524288
  186.8 8.8 %reshape.220 = f32[8192,8]{1,0:T(8,128)} reshape(f32[8192,2,4]{2,1,0:T(2,128)} %bitcast.140) | data formatting | bytes 524288
  195.7 61.1 %reduce-scatter.7.cloned.1.call-done = f32[1024,8]{1,0:T(8,128)} async-done(((f32[4096,8]{1,0:T(8,128)}), f32[1024,8]{1,0:T(8,128)}) %reduce-scatter.7.cloned.1.call-update) | async-done | bytes 32784
  256.7 1.6 reshape.219
  258.8 50.3 %reduce-scatter.9.cloned.1.call-done = f32[1024,8]{1,0:T(8,128)} async-done(((f32[8192,8]{1,0:T(8,128)}), f32[1024,8]{1,0:T(8,128)}) %reduce-scatter.9.cloned.1.call-update) | async-done | bytes 32784
  309.2 1.6 reshape.221
  312.2 26.6 %scatter_fusion = f32[2,4,1024]{1,0,2:T(2,128)S(1)} fusion(f32[2,4,1024]{1,0,2:T(2,128)S(1)} %broadcast_in_dim.55, s32[1024]{0:T(1024)S(1)} %bitcast.151, f32[1024,2,4]{2,1,0:T(2,128)S(1)} %copy.48), kind=kCustom, calls=%fused_computation.6 | custom fusion | bytes 102400 | tf_op jit(solution)/shard_map/scatter | solution.py:122
  338.8 1.1 copy.49
  (190 shorter events, 47.3 us)
Async XLA Ops:
  6.5 250.2 %reduce-scatter.7.cloned.1.call-start = ((), (), s32[]{:S(2)}) async-start(), calls=%async_computation.2 | async-start | bytes 2621440
  73.5 0.7 copy-start.2
  73.5 2.1 copy-start
  178.0 0.9 copy-start.1
  178.0 131.2 %reduce-scatter.9.cloned.1.call-start = ((), (), s32[]{:S(2)}) async-start(), calls=%async_computation.3 | async-start | bytes 4718592
Sparse Core Ops, SparseCore 0:
  178.1 78.5 reduce-scatter.6
  259.1 50.0 reduce-scatter.8
where the time goes:
time: 348 us; the launch traced here: 347 us
  waiting for transfers between devices  111 us (32%)
  local copies, waits for them, and re-layouts  108 us (31%)
  blocking collectives  57.2 us (16%)
  other arithmetic  32.9 us (9%)
  between operations  14.2 us (4%)
  matrix products  11.7 us (3%)
  loops' own time  10.7 us (3%)
    unnamed x4, waiting for transfers between devices  111 us
    all_gather x1, blocking collectives, body(): col_data = lax.all_gather(ordered, ('row', 'sub'), axis=1, tiled=True)  41.4 us
    unnamed x14, local copies, waits for them, and re-layouts  32.4 us
    scatter x2, local copies, waits for them, and re-layouts, body(): return jnp.zeros_like(combined).at[:, :, cluster_panels[0]].set(combined)  27.7 us
    gather x48, local copies, waits for them, and re-layouts  19.5 us
    all_gather x1, blocking collectives, body(): row_data = lax.all_gather(ordered, ('col', 'sub'), axis=1, tiled=True)  15.8 us
    another operation x1, loops' own time, body(): row_sums, col_sums = lax.fori_loop(0, turn_count, one_turn, start_sums)  10.7 us
    dynamic_update_slice x8, other arithmetic, one_turn(): lax.dynamic_update_slice_in_dim(col_sums, current + onto_col[member], col...  10.5 us
  transfers between devices with their start and end apart: 2, of which 2 were waited for; matrix products, arithmetic and copies ran while one was open for 5% of the time, Pallas kernels for 0%

commit v1 on v0

v1 whole, which is shorter than its diff:
```python
import functools
import math

import jax
import jax.numpy as jnp
import numpy as np
from jax import lax
from jax.experimental import pallas as pl
from jax.experimental.pallas import tpu as pltpu
from jax.sharding import PartitionSpec as P

MESH = pl.DeviceIdType.MESH
PANEL = 256
HALF = 128
WAVENUMBER = 3.0
SOFTEN = 0.5
FOUR_PI = 4.0 * math.pi
F32 = jnp.float32
BF16 = jnp.bfloat16
CHUNK = 16


def fit(func, degree):
    cheb = np.polynomial.chebyshev.Chebyshev.interpolate(func, degree, domain=[0.0, 0.2501])
    return [float(v) for v in cheb.convert(kind=np.polynomial.Polynomial).coef]


def sinc_turn(z):
    f = np.sqrt(np.maximum(z, 1e-30))
    return np.sin(2 * np.pi * f) / f


COS_COEF = [v / FOUR_PI for v in fit(lambda z: np.cos(2 * np.pi * np.sqrt(np.maximum(z, 0.0))), 6)]
SIN_COEF = [v * WAVENUMBER / FOUR_PI for v in fit(sinc_turn, 6)]


def horner(coef, z):
    value = coef[-1] * z + coef[-2]
    for c in coef[-3::-1]:
        value = value * z + c
    return value


def two_parts(value):
    hi = value.astype(BF16)
    lo = (value - hi.astype(F32)).astype(BF16)
    return hi, lo


def three_parts(value):
    hi = value.astype(BF16).astype(F32)
    rest = value - hi
    mid = rest.astype(BF16).astype(F32)
    return jnp.concatenate([hi, mid, rest - mid], axis=0)


def tile_parts(e, n_i, n_j, soften_sq):
    rho_sq = e[0] * e[0] + e[1] * e[1] + e[2] * e[2] + soften_sq
    inv = lax.rsqrt(rho_sq)
    rho = rho_sq * inv
    turns = rho * (WAVENUMBER / (2 * math.pi))
    f = turns - jnp.round(turns)
    z = f * f
    cosine = horner(COS_COEF, z)
    radial = (cosine + rho * f * horner(SIN_COEF, z)) * (inv * inv * inv)
    double = radial * (e[0] * n_j[0] + e[1] * n_j[1] + e[2] * n_j[2])
    adjoint = radial * (e[0] * n_i[0] + e[1] * n_i[1] + e[2] * n_i[2])
    return cosine * inv, double, adjoint


def kernel(
    sizes,
    dens_ref, pos_ref, nrm_ref, wgt_ref, order_ref, pair_ref, quad_ref, count_ref,
    out_ref,
    onehot, stacked, meta, meta_s, row_buf, col_half, col_buf,
    tiles, row_term, col_term, row_send, col_send, row_recv, col_recv,
    meta_sem, local_sem, row_ssem, row_rsem, col_ssem, col_rsem,
    row_ssem2, row_rsem2, col_ssem2, col_rsem2,
):
    n_row, n_col, n_sub, cl_dev, slots, used = sizes
    own = cl_dev * PANEL
    row_devs = n_col * n_sub
    col_devs = n_row * n_sub
    r = lax.axis_index("row")
    c = lax.axis_index("col")
    s = lax.axis_index("sub")
    me_row = c * n_sub + s
    me_col = r * n_sub + s

    def row_peer(d):
        idx = lax.rem(me_row + d, row_devs)
        return idx, {"col": idx // n_sub, "sub": lax.rem(idx, n_sub)}

    def col_peer(d):
        idx = lax.rem(me_col + d, col_devs)
        return idx, {"row": idx // n_sub, "sub": lax.rem(idx, n_sub)}

    barrier = pltpu.get_barrier_semaphore()
    for d in range(1, row_devs):
        pl.semaphore_signal(barrier, inc=1, device_id=row_peer(d)[1], device_id_type=MESH)
    for d in range(1, col_devs):
        pl.semaphore_signal(barrier, inc=1, device_id=col_peer(d)[1], device_id_type=MESH)

    def fill(t, carry):
        base = pl.multiple_of(t * 64, 64)
        ids = lax.broadcasted_iota(jnp.int32, (64, own), 0) + base
        onehot[pl.ds(base, 64), :] = jnp.where(ids == order_ref[...], 1.0, 0.0).astype(BF16)
        return carry

    lax.fori_loop(0, own // 64, fill, 0)

    stacked[0:3, :] = pos_ref[...]
    stacked[3:6, :] = nrm_ref[...]
    stacked[6:8, :] = jnp.zeros((2, own), F32)
    stacked[8:12, :] = dens_ref[0] * wgt_ref[...]
    stacked[12:16, :] = dens_ref[1]
    meta[0] = jnp.zeros((8, 128), jnp.int32)
    meta[0, 0:2, 0:slots] = pair_ref[...]
    meta[0, 2:3, 0:slots] = quad_ref[...]
    meta[0, 3:4, 0:1] = count_ref[...]
    parts = three_parts(stacked[...]).astype(BF16)
    for g in range(cl_dev):
        got = jnp.dot(parts, onehot[:, g * PANEL : (g + 1) * PANEL], preferred_element_type=F32)
        panels = (got[0:16] + got[16:32]) + got[32:48]
        row_buf[me_row * cl_dev + g] = panels
        for h in range(2):
            col_half[h, g] = panels[:, h * HALF : (h + 1) * HALF]
    col_buf[pl.ds(me_col * cl_dev, cl_dev)] = col_half[s]

    pl.semaphore_wait(barrier, row_devs + col_devs - 2)

    other = 1 - s
    meta_copy = pltpu.make_async_remote_copy(
        src_ref=meta.at[0], dst_ref=meta.at[1], send_sem=meta_sem.at[0], recv_sem=meta_sem.at[1],
        device_id={"sub": other}, device_id_type=MESH,
    )
    meta_copy.start()

    def col_copy(d):
        idx, dev = col_peer(d)
        there = pl.ds(me_col * cl_dev, cl_dev)
        return pltpu.make_async_remote_copy(
            src_ref=col_half.at[dev["sub"]], dst_ref=col_buf.at[there],
            send_sem=col_ssem.at[d], recv_sem=col_rsem.at[d],
            device_id=dev, device_id_type=MESH,
        )

    def row_copy(d):
        idx, dev = row_peer(d)
        here = pl.ds(me_row * cl_dev, cl_dev)
        return pltpu.make_async_remote_copy(
            src_ref=row_buf.at[here], dst_ref=row_buf.at[here],
            send_sem=row_ssem.at[d], recv_sem=row_rsem.at[d],
            device_id=dev, device_id_type=MESH,
        )

    def col_arrived(d):
        idx = lax.rem(me_col + col_devs - d, col_devs)
        here = pl.ds(idx * cl_dev, cl_dev)
        pltpu.make_async_remote_copy(
            src_ref=col_half.at[0], dst_ref=col_buf.at[here],
            send_sem=col_ssem.at[d], recv_sem=col_rsem.at[d],
            device_id={"sub": other}, device_id_type=MESH,
        ).wait_recv()

    def row_arrived(d):
        idx = lax.rem(me_row + row_devs - d, row_devs)
        here = pl.ds(idx * cl_dev, cl_dev)
        pltpu.make_async_remote_copy(
            src_ref=row_buf.at[here], dst_ref=row_buf.at[here],
            send_sem=row_ssem.at[d], recv_sem=row_rsem.at[d],
            device_id={"sub": other}, device_id_type=MESH,
        ).wait_recv()

    for d in range(1, col_devs):
        col_copy(d).start()
    for d in range(1, row_devs):
        row_copy(d).start()

    meta_copy.wait()
    to_smem = pltpu.make_async_copy(meta, meta_s, local_sem)
    to_smem.start()
    to_smem.wait()
    for d in range(1, row_devs):
        row_arrived(d)
    for d in range(1, col_devs):
        col_arrived(d)

    first_rows = lax.broadcasted_iota(jnp.int32, (8, HALF), 0) < 4
    first_rows_wide = lax.broadcasted_iota(jnp.int32, (8, PANEL), 0) < 4

    def slot_of(k):
        count0 = jnp.where(s == 0, meta_s[0, 3, 0], meta_s[1, 3, 0])
        is_first = k < count0
        bank = jnp.where(is_first, s, 1 - s)
        at = jnp.where(is_first, k, k - count0)
        return meta_s[bank, 0, at], meta_s[bank, 1, at], meta_s[bank, 2, at]

    def swap(v):
        return jnp.concatenate([v[4:8], v[0:4]], axis=0)

    def one_slot(k, carry):
        v, u, q = slot_of(k)
        x_i = row_buf[v]
        y_j = col_buf[u]
        q_f = jnp.full((1, PANEL), q, jnp.int32).astype(F32)
        soften_sq = (SOFTEN / q_f) * (SOFTEN / q_f)
        t_j = jnp.transpose(y_j[0:8])
        for m in range(HALF // CHUNK):
            at = slice(m * CHUNK, (m + 1) * CHUNK)
            e = [x_i[a : a + 1] - t_j[at, a : a + 1] for a in range(3)]
            n_i = [x_i[3 + a : 4 + a] for a in range(3)]
            n_j = [t_j[at, 3 + a : 4 + a] for a in range(3)]
            for b, value in enumerate(tile_parts(e, n_i, n_j, soften_sq)):
                hi, lo = two_parts(value)
                tiles[b * 2 * HALF + m * CHUNK : b * 2 * HALF + (m + 1) * CHUNK, :] = hi
                tiles[b * 2 * HALF + HALF + m * CHUNK : b * 2 * HALF + HALF + (m + 1) * CHUNK, :] = lo
        d_j = y_j[8:16]
        s_j = swap(d_j)
        sig = jnp.where(first_rows, d_j, 0.0)
        mu = jnp.where(first_rows, s_j, 0.0)
        adj = jnp.where(first_rows, 0.0, -s_j)

        def stack_parts(value):
            hi = value.astype(BF16).astype(F32)
            return jnp.concatenate([hi, value - hi], axis=0).astype(BF16)

        sig, mu, adj = stack_parts(sig), stack_parts(mu), stack_parts(adj)
        lhs = jnp.concatenate([sig, sig, mu, mu, adj, adj], axis=1)
        got = jnp.dot(lhs, tiles[...], preferred_element_type=F32)
        row_term[k] = got[0:8] + got[8:16]
        lhs = stack_parts(x_i[8:16])
        got = lax.dot_general(lhs, tiles[...], (((1,), (1,)), ((), ())), preferred_element_type=F32)
        got = got[0:8] + got[8:16]
        t = [got[:, b * 2 * HALF : b * 2 * HALF + HALF] + got[:, b * 2 * HALF + HALF : (b + 1) * 2 * HALF] for b in range(3)]
        col_term[k] = jnp.where(first_rows, t[0] - swap(t[2]), swap(t[1]))
        return carry

    lax.fori_loop(0, used, one_slot, 0)

    slot_info = [slot_of(k) for k in range(used)]
    row_ids = [info[0] for info in slot_info]
    col_ids = []
    for v, u, _ in slot_info:
        a = r * (cl_dev * row_devs) + v
        per = n_sub * cl_dev
        b = ((u // per * n_col + c) * n_sub + lax.rem(u // cl_dev, n_sub)) * cl_dev + lax.rem(u, cl_dev)
        col_ids.append(jnp.where(a == b, -1, u))

    def col_sum(idx, g):
        total = jnp.zeros((8, HALF), F32)
        for k in range(used):
            total += jnp.where(col_ids[k] == idx * cl_dev + g, col_term[k], 0.0)
        return total

    def row_sum(idx, g):
        total = jnp.zeros((8, PANEL), F32)
        for k in range(used):
            total += jnp.where(row_ids[k] == idx * cl_dev + g, row_term[k], 0.0)
        return total

    def col_back(d):
        idx, dev = col_peer(d)
        return pltpu.make_async_remote_copy(
            src_ref=col_send.at[d], dst_ref=col_recv.at[me_col],
            send_sem=col_ssem2.at[d], recv_sem=col_rsem2.at[d],
            device_id=dev, device_id_type=MESH,
        )

    def row_back(d):
        idx, dev = row_peer(d)
        return pltpu.make_async_remote_copy(
            src_ref=row_send.at[d], dst_ref=row_recv.at[me_row],
            send_sem=row_ssem2.at[d], recv_sem=row_rsem2.at[d],
            device_id=dev, device_id_type=MESH,
        )

    def send_col(d, carry):
        for g in range(cl_dev):
            col_send[d, g] = col_sum(col_peer(d)[0], g)
        col_back(d).start()
        return carry

    def send_row(d, carry):
        for g in range(cl_dev):
            row_send[d, g] = row_sum(row_peer(d)[0], g)
        row_back(d).start()
        return carry

    lax.fori_loop(1, col_devs, send_col, 0)
    lax.fori_loop(1, row_devs, send_row, 0)
    for g in range(cl_dev):
        col_recv[me_col, g] = col_sum(me_col, g)
        row_recv[me_row, g] = row_sum(me_row, g)

    for d in range(1, row_devs):
        row_copy(d).wait_send()
    for d in range(1, col_devs):
        col_copy(d).wait_send()
    for d in range(1, row_devs):
        idx = lax.rem(me_row + row_devs - d, row_devs)
        pltpu.make_async_remote_copy(
            src_ref=row_send.at[d], dst_ref=row_recv.at[idx],
            send_sem=row_ssem2.at[d], recv_sem=row_rsem2.at[d],
            device_id={"sub": other}, device_id_type=MESH,
        ).wait_recv()
    for d in range(1, col_devs):
        idx = lax.rem(me_col + col_devs - d, col_devs)
        pltpu.make_async_remote_copy(
            src_ref=col_send.at[d], dst_ref=col_recv.at[idx],
            send_sem=col_ssem2.at[d], recv_sem=col_rsem2.at[d],
            device_id={"sub": other}, device_id_type=MESH,
        ).wait_recv()

    pieces = []
    for g in range(cl_dev):
        for h in range(2):
            total = row_recv[0, g, :, h * HALF : (h + 1) * HALF]
            for idx in range(1, row_devs):
                total += row_recv[idx, g, :, h * HALF : (h + 1) * HALF]
            for rr in range(n_row):
                total += col_recv[rr * n_sub + h, g]
            pieces.append(total)
    combined = jnp.concatenate(pieces, axis=1)
    parts = jnp.concatenate([three_parts(combined), jnp.zeros((8, own), F32)], axis=0).astype(BF16)
    for g in range(cl_dev):
        at = slice(g * PANEL, (g + 1) * PANEL)
        got = lax.dot_general(parts, onehot[at, :], (((1,), (1,)), ((), ())), preferred_element_type=F32)
        got = (got[0:8] + got[8:16]) + got[16:24]
        out_ref[0, :, at] = got[0:4] * wgt_ref[:, at]
        out_ref[1, :, at] = got[4:8]

    for d in range(1, row_devs):
        row_back(d).wait_send()
    for d in range(1, col_devs):
        col_back(d).wait_send()


def body(densities, positions, normals, weights, cluster_panels, pair_list, quad_order, pair_count):
    n_row, n_col, n_sub = (lax.axis_size(a) for a in ("row", "col", "sub"))
    own = positions.shape[1]
    cl_dev = own // PANEL
    slots = pair_list.shape[1]
    used = slots + slots // 4
    row_devs = n_col * n_sub
    col_devs = n_row * n_sub
    sizes = (n_row, n_col, n_sub, cl_dev, slots, used)
    dma = pltpu.SemaphoreType.DMA
    vmem = pltpu.VMEM
    return pl.pallas_call(
        functools.partial(kernel, sizes),
        out_shape=jax.ShapeDtypeStruct(densities.shape, F32),
        in_specs=[pl.BlockSpec(memory_space=pltpu.VMEM)] * 8,
        out_specs=pl.BlockSpec(memory_space=pltpu.VMEM),
        scratch_shapes=[
            vmem((own, own), BF16),
            vmem((16, own), F32),
            vmem((2, 8, 128), jnp.int32),
            pltpu.SMEM((2, 8, 128), jnp.int32),
            vmem((row_devs * cl_dev, 16, PANEL), F32),
            vmem((2, cl_dev, 16, HALF), F32),
            vmem((col_devs * cl_dev, 16, HALF), F32),
            vmem((6 * HALF, PANEL), BF16),
            vmem((used, 8, PANEL), F32),
            vmem((used, 8, HALF), F32),
            vmem((row_devs, cl_dev, 8, PANEL), F32),
            vmem((col_devs, cl_dev, 8, HALF), F32),
            vmem((row_devs, cl_dev, 8, PANEL), F32),
            vmem((col_devs, cl_dev, 8, HALF), F32),
            dma((2,)),
            dma,
            dma((row_devs,)), dma((row_devs,)), dma((col_devs,)), dma((col_devs,)),
            dma((row_devs,)), dma((row_devs,)), dma((col_devs,)), dma((col_devs,)),
        ],
        compiler_params=pltpu.CompilerParams(
            collective_id=0, has_side_effects=True, vmem_limit_bytes=40 * 1024 * 1024
        ),
    )(
        densities, positions, normals, weights.reshape(1, own), cluster_panels,
        pair_list, quad_order.reshape(1, slots), pair_count.reshape(1, 1),
    )


def solution(mesh):
    split = ("groups", "row", "col", "sub")
    placed = (
        P(None, None, split), P(None, split), P(None, split), P(split),
        P(split, None), P(None, split), P(split), P(split),
    )
    return jax.shard_map(
        body, mesh=mesh, in_specs=placed, out_specs=P(None, None, split), check_vma=False
    )
```

time: 348 us -> 32.8 us (0.09)
  waiting for transfers between devices: 111 us -> 0 us
  local copies, waits for them, and re-layouts: 108 us -> 4.16 us
  blocking collectives: 57.2 us -> 0 us
  other arithmetic: 32.9 us -> 0 us
  Pallas kernels: 0 us -> 27.5 us
  between operations: 14.2 us -> 0.7 us
  matrix products: 11.7 us -> 0 us
  loops' own time: 10.7 us -> 0 us
    unnamed x4 -> x0, waiting for transfers between devices: 111 us -> none
    all_gather x2 -> x0, blocking collectives: 57.2 us -> none  [the longest x1 41.4 us: body(): col_data = lax.all_gather(ordered, ('row', 'sub'), axis=1, tiled=True)]
    gather x69 -> x0, local copies, waits for them, and re-layouts: 35.1 us -> none
    unnamed x14 -> x15, local copies, waits for them, and re-layouts: 32.4 us -> 4.16 us
    scatter x2 -> x0, local copies, waits for them, and re-layouts: 27.7 us -> none  [body(): return jnp.zeros_like(combined).at[:, :, cluster_panels[0]].set(combined)]
    pallas_call x0 -> x1, Pallas kernels: none -> 27.5 us  [body(): pl.pallas_call(functools.partial(kernel, sizes), out_shape=jax.ShapeDtype...]
    dynamic_update_slice x12 -> x0, other arithmetic: 15.7 us -> none  [the longest x8 10.5 us: one_turn(): lax.dynamic_update_slice_in_dim(col_sums, current + onto_col[member], col...]
    dot_general x24 -> x0, matrix products: 11.7 us -> none  [the longest x12 6.77 us: apply_rows(): return jnp.einsum('ij,rj->ri', tile, dens, precision=lax.Precision.HIGHEST)]
  transfers between devices with their start and end apart: 2 -> 0, of which waited for: 2 -> 0; matrix products, arithmetic and copies ran while one was open for 5% -> 0% of each run, Pallas kernels for 0% -> 0%
where the time goes in v1:
time: 32.8 us; the launch traced here: 32.4 us
  Pallas kernels  27.5 us (84%)
  local copies, waits for them, and re-layouts  4.16 us (13%)
  between operations  0.7 us (2%)
    pallas_call x1, Pallas kernels, body(): pl.pallas_call(functools.partial(kernel, sizes), out_shape=jax.ShapeDtype...  27.5 us
    unnamed x15, local copies, waits for them, and re-layouts  4.16 us

profile of v1, /device:TPU:0, one launch (start us, length us, event | category | flops | bytes accessed | tf_op | source)
XLA Modules:
  0.0 32.4 jit_solution(8716931954770201368)
XLA Ops:
  0.0 0.0 copy-start.3
  0.7 0.0 copy-start.5
  0.7 0.0 copy-start.6
  0.7 0.0 copy-done.3
  0.7 0.7 %copy-done.5 = s32[2,12]{1,0:T(2,128)S(1)} copy-done((s32[2,12]{1,0:T(2,128)S(1)}, s32[2,12]{1,0:T(2,128)}, u32[]{:S(2)}) %copy-start.5) | copy-done | bytes 120
  1.3 0.0 copy-done.6
  1.4 0.0 copy-start
  1.4 0.8 %copy-done = f32[2,4,1024]{2,1,0:T(4,128)S(1)} copy-done((f32[2,4,1024]{2,1,0:T(4,128)S(1)}, f32[2,4,1024]{2,1,0:T(4,128)}, u32[]{:S(2)}) %copy-start) | copy-done | bytes 32792
  2.1 0.0 copy-start.1
  2.1 0.7 %copy-done.1 = f32[3,1024]{1,0:T(4,128)S(1)} copy-done((f32[3,1024]{1,0:T(4,128)S(1)}, f32[3,1024]{1,0:T(4,128)}, u32[]{:S(2)}) %copy-start.1) | copy-done | bytes 12312
  2.8 0.0 copy-start.2
  2.8 0.7 %copy-done.2 = f32[3,1024]{1,0:T(4,128)S(1)} copy-done((f32[3,1024]{1,0:T(4,128)S(1)}, f32[3,1024]{1,0:T(4,128)}, u32[]{:S(2)}) %copy-start.2) | copy-done | bytes 12312
  3.5 0.0 copy-start.4
  3.5 0.7 %copy-done.4 = s32[1,1024]{1,0:T(1,128)S(1)} copy-done((s32[1,1024]{1,0:T(1,128)S(1)}, s32[1,1024]{1,0:T(1,128)}, u32[]{:S(2)}) %copy-start.4) | copy-done | bytes 4120
  4.2 27.5 %shard_map.82 = f32[2,4,1024]{2,1,0:T(4,128)S(1)} custom-call(f32[2,4,1024]{2,1,0:T(4,128)S(1)} %copy-done, f32[3,1024]{1,0:T(4,128)S(1)} %copy-done.1, f32[3,1024]{1,0:T(4,128)S(1)} %copy-done.2, f32[1,1024]{1,0:T(1,128)S(1)} %bitcast.4, s32[1,1024]{1,0:T(1,128)S(1)} %copy-done.4, s32[2,12]{1,0:T(2,128)S(1)} %copy-done.5, s32[1,12]{1,0:T(1,128)S(1)} %bitcast.5, ...), custom_call_target="tpu_custom_call" | custom-call | tf_op jit(solution)/shard_map/pallas_call | solution.py:350
  31.8 0.6 %copy.11 = f32[2,4,1024]{2,1,0:T(4,128)} copy(f32[2,4,1024]{2,1,0:T(4,128)S(1)} %shard_map.82) | data formatting | bytes 65536
Async XLA Ops:
  0.0 0.7 %copy-start.3 = (f32[1024]{0:T(1024)S(1)}, f32[1024]{0:T(1024)}, u32[]{:S(2)}) copy-start(f32[1024]{0:T(1024)} %param.11) | copy-start | bytes 12292
  0.7 0.7 %copy-start.5 = (s32[2,12]{1,0:T(2,128)S(1)}, s32[2,12]{1,0:T(2,128)}, u32[]{:S(2)}) copy-start(s32[2,12]{1,0:T(2,128)} %pair_ref.1) | copy-start | bytes 292
  0.7 0.7 %copy-start.6 = (s32[12]{0:T(128)S(1)}, s32[12]{0:T(128)}, u32[]{:S(2)}) copy-start(s32[12]{0:T(128)} %param.14) | copy-start | bytes 148
  1.4 0.8 %copy-start = (f32[2,4,1024]{2,1,0:T(4,128)S(1)}, f32[2,4,1024]{2,1,0:T(4,128)}, u32[]{:S(2)}) copy-start(f32[2,4,1024]{2,1,0:T(4,128)} %dens_ref.1) | copy-start | bytes 98308
  2.1 0.7 %copy-start.1 = (f32[3,1024]{1,0:T(4,128)S(1)}, f32[3,1024]{1,0:T(4,128)}, u32[]{:S(2)}) copy-start(f32[3,1024]{1,0:T(4,128)} %pos_ref.1) | copy-start | bytes 36868
  2.8 0.7 %copy-start.2 = (f32[3,1024]{1,0:T(4,128)S(1)}, f32[3,1024]{1,0:T(4,128)}, u32[]{:S(2)}) copy-start(f32[3,1024]{1,0:T(4,128)} %nrm_ref.1) | copy-start | bytes 36868
  3.5 0.7 %copy-start.4 = (s32[1,1024]{1,0:T(1,128)S(1)}, s32[1,1024]{1,0:T(1,128)}, u32[]{:S(2)}) copy-start(s32[1,1024]{1,0:T(1,128)} %order_ref.1) | copy-start | bytes 12292

commit v2 on v1

--- a/solution.py
+++ b/solution.py
@@ -70,8 +70,9 @@
 
 def kernel(
     sizes,
-    dens_ref, pos_ref, nrm_ref, wgt_ref, order_ref, pair_ref, quad_ref, count_ref,
+    dens_in, pos_in, nrm_in, wgt_in, order_in, pair_in, quad_in, count_in,
     out_ref,
+    dens_ref, pos_ref, nrm_ref, wgt_ref, order_ref, pair_ref, quad_ref, count_ref, in_sem,
     onehot, stacked, meta, meta_s, row_buf, col_half, col_buf,
     tiles, row_term, col_term, row_send, col_send, row_recv, col_recv,
     meta_sem, local_sem, row_ssem, row_rsem, col_ssem, col_rsem,
@@ -95,12 +96,22 @@
         idx = lax.rem(me_col + d, col_devs)
         return idx, {"row": idx // n_sub, "sub": lax.rem(idx, n_sub)}
 
+    loads = [
+        pltpu.make_async_copy(src, dst, in_sem.at[n])
+        for n, (src, dst) in enumerate((
+            (order_in, order_ref), (wgt_in, wgt_ref), (dens_in, dens_ref), (pos_in, pos_ref),
+            (nrm_in, nrm_ref), (pair_in, pair_ref), (quad_in, quad_ref), (count_in, count_ref),
+        ))
+    ]
+    for load in loads:
+        load.start()
     barrier = pltpu.get_barrier_semaphore()
     for d in range(1, row_devs):
         pl.semaphore_signal(barrier, inc=1, device_id=row_peer(d)[1], device_id_type=MESH)
     for d in range(1, col_devs):
         pl.semaphore_signal(barrier, inc=1, device_id=col_peer(d)[1], device_id_type=MESH)
 
+    loads[0].wait()
     def fill(t, carry):
         base = pl.multiple_of(t * 64, 64)
         ids = lax.broadcasted_iota(jnp.int32, (64, own), 0) + base
@@ -109,6 +120,8 @@
 
     lax.fori_loop(0, own // 64, fill, 0)
 
+    for load in loads[1:]:
+        load.wait()
     stacked[0:3, :] = pos_ref[...]
     stacked[3:6, :] = nrm_ref[...]
     stacked[6:8, :] = jnp.zeros((2, own), F32)
@@ -350,9 +363,18 @@
     return pl.pallas_call(
         functools.partial(kernel, sizes),
         out_shape=jax.ShapeDtypeStruct(densities.shape, F32),
-        in_specs=[pl.BlockSpec(memory_space=pltpu.VMEM)] * 8,
+        in_specs=[pl.BlockSpec(memory_space=pltpu.HBM)] * 8,
         out_specs=pl.BlockSpec(memory_space=pltpu.VMEM),
         scratch_shapes=[
+            vmem(densities.shape, F32),
+            vmem((3, own), F32),
+            vmem((3, own), F32),
+            vmem((1, own), F32),
+            vmem((1, own), jnp.int32),
+            vmem((2, slots), jnp.int32),
+            vmem((1, slots), jnp.int32),
+            vmem((1, 1), jnp.int32),
+            dma((8,)),
             vmem((own, own), BF16),
             vmem((16, own), F32),
             vmem((2, 8, 128), jnp.int32),
@@ -373,7 +395,7 @@
             dma((row_devs,)), dma((row_devs,)), dma((col_devs,)), dma((col_devs,)),
         ],
         compiler_params=pltpu.CompilerParams(
-            collective_id=0, has_side_effects=True, vmem_limit_bytes=40 * 1024 * 1024
+            collective_id=0, has_side_effects=True, vmem_limit_bytes=60 * 1024 * 1024
         ),
     )(
         densities, positions, normals, weights.reshape(1, own), cluster_panels,

time: 32.8 us -> 30.6 us (0.933)
  local copies, waits for them, and re-layouts: 4.16 us -> 1.38 us
  Pallas kernels: 27.5 us -> 28.3 us
    unnamed x15 -> x1, local copies, waits for them, and re-layouts: 4.16 us -> 1.38 us
    pallas_call x1, Pallas kernels: 27.5 us -> 28.3 us  [body(): pl.pallas_call(functools.partial(kernel, sizes), out_shape=jax.ShapeDtype...]
where the time goes in v2:
time: 30.6 us; the launch traced here: 30.4 us
  Pallas kernels  28.3 us (92%)
  local copies, waits for them, and re-layouts  1.38 us (5%)
  between operations  0.66 us (2%)
    pallas_call x1, Pallas kernels, body(): pl.pallas_call(functools.partial(kernel, sizes), out_shape=jax.ShapeDtype...  28.3 us
    unnamed x1, local copies, waits for them, and re-layouts  1.38 us

profile of v2, /device:TPU:0, one launch (start us, length us, event | category | flops | bytes accessed | tf_op | source)
XLA Modules:
  0.0 30.4 jit_solution(6222128658974970245)
XLA Ops:
  0.7 28.3 %shard_map.82 = f32[2,4,1024]{2,1,0:T(4,128)} custom-call(f32[2,4,1024]{2,1,0:T(4,128)} %dens_in.1, f32[3,1024]{1,0:T(4,128)} %pos_in.1, f32[3,1024]{1,0:T(4,128)} %nrm_in.1, f32[1,1024]{1,0:T(1,128)} %bitcast.4, s32[1,1024]{1,0:T(1,128)} %order_in.1, s32[2,12]{1,0:T(2,128)} %pair_in.1, s32[1,12]{1,0:T(1,128)} %bitcast.5, s32[1,1]{1,0:T(1,128)} %bitcast.3.count_in), custom_call_target="tpu_custom_call" | custom-call | tf_op jit(solution)/shard_map/pallas_call | solution.py:363
  29.0 1.4 %copy.11 = f32[2,4,1024]{2,1,0:T(4,128)} copy(f32[2,4,1024]{2,1,0:T(4,128)} %shard_map.82) | data formatting | bytes 65536

commit v3 on v2

--- a/solution.py
+++ b/solution.py
@@ -30,8 +30,8 @@
     return np.sin(2 * np.pi * f) / f
 
 
-COS_COEF = [v / FOUR_PI for v in fit(lambda z: np.cos(2 * np.pi * np.sqrt(np.maximum(z, 0.0))), 6)]
-SIN_COEF = [v * WAVENUMBER / FOUR_PI for v in fit(sinc_turn, 6)]
+COS_COEF = [v / FOUR_PI for v in fit(lambda z: np.cos(2 * np.pi * np.sqrt(np.maximum(z, 0.0))), 5)]
+SIN_COEF = [v * WAVENUMBER / FOUR_PI for v in fit(sinc_turn, 5)]
 
 
 def horner(coef, z):
@@ -54,7 +54,7 @@
     return jnp.concatenate([hi, mid, rest - mid], axis=0)
 
 
-def tile_parts(e, n_i, n_j, soften_sq):
+def tile_parts(e, along_col, along_row, soften_sq):
     rho_sq = e[0] * e[0] + e[1] * e[1] + e[2] * e[2] + soften_sq
     inv = lax.rsqrt(rho_sq)
     rho = rho_sq * inv
@@ -63,9 +63,7 @@
     z = f * f
     cosine = horner(COS_COEF, z)
     radial = (cosine + rho * f * horner(SIN_COEF, z)) * (inv * inv * inv)
-    double = radial * (e[0] * n_j[0] + e[1] * n_j[1] + e[2] * n_j[2])
-    adjoint = radial * (e[0] * n_i[0] + e[1] * n_i[1] + e[2] * n_i[2])
-    return cosine * inv, double, adjoint
+    return cosine * inv, radial * along_col, radial * along_row
 
 
 def kernel(
@@ -74,12 +72,13 @@
     out_ref,
     dens_ref, pos_ref, nrm_ref, wgt_ref, order_ref, pair_ref, quad_ref, count_ref, in_sem,
     onehot, stacked, meta, meta_s, row_buf, col_half, col_buf,
-    tiles, row_term, col_term, row_send, col_send, row_recv, col_recv,
+    tiles_a, tiles_b, tiles_c, row_term, col_term, row_send, col_send, row_recv, col_recv,
     meta_sem, local_sem, row_ssem, row_rsem, col_ssem, col_rsem,
     row_ssem2, row_rsem2, col_ssem2, col_rsem2,
 ):
     n_row, n_col, n_sub, cl_dev, slots, used = sizes
     own = cl_dev * PANEL
+    tile_bufs = (tiles_a, tiles_b, tiles_c)
     row_devs = n_col * n_sub
     col_devs = n_row * n_sub
     r = lax.axis_index("row")
@@ -212,19 +211,44 @@
     def swap(v):
         return jnp.concatenate([v[4:8], v[0:4]], axis=0)
 
-    def one_slot(k, carry):
+    def split3(value):
+        hi = value.astype(BF16).astype(F32)
+        rest = value - hi
+        mid = rest.astype(BF16).astype(F32)
+        return hi, mid, rest - mid
+
+    def left_parts(value):
+        hi, mid, lo = split3(value)
+        return jnp.concatenate([hi, hi, mid, hi, mid, lo], axis=0)
+
+    def right_parts(value):
+        hi, mid, lo = split3(value)
+        return jnp.concatenate([hi, mid, hi, lo, mid, hi], axis=0)
+
+    def dot3(a, b):
+        return a[0:1] * b[0:1] + a[1:2] * b[1:2] + a[2:3] * b[2:3]
+
+    def one_slot(k, tiles):
         v, u, q = slot_of(k)
         x_i = row_buf[v]
         y_j = col_buf[u]
         q_f = jnp.full((1, PANEL), q, jnp.int32).astype(F32)
         soften_sq = (SOFTEN / q_f) * (SOFTEN / q_f)
+        x_in, n_in = x_i[0:3], x_i[3:6]
+        x_jn, n_jn = y_j[0:3], y_j[3:6]
+        pad_i, pad_j = jnp.zeros((4, PANEL), F32), jnp.zeros((4, HALF), F32)
+        one_i, one_j = jnp.ones((1, PANEL), F32), jnp.ones((1, HALF), F32)
+        to_col_l = left_parts(jnp.concatenate([n_jn, -dot3(x_jn, n_jn), pad_j], axis=0))
+        to_row_l = left_parts(jnp.concatenate([-x_jn, one_j, pad_j], axis=0))
+        to_col_r = right_parts(jnp.concatenate([x_in, one_i, pad_i], axis=0)).astype(BF16)
+        to_row_r = right_parts(jnp.concatenate([n_in, dot3(x_in, n_in), pad_i], axis=0)).astype(BF16)
         t_j = jnp.transpose(y_j[0:8])
+        along_col = jnp.dot(jnp.transpose(to_col_l).astype(BF16), to_col_r, preferred_element_type=F32)
+        along_row = jnp.dot(jnp.transpose(to_row_l).astype(BF16), to_row_r, preferred_element_type=F32)
         for m in range(HALF // CHUNK):
             at = slice(m * CHUNK, (m + 1) * CHUNK)
             e = [x_i[a : a + 1] - t_j[at, a : a + 1] for a in range(3)]
-            n_i = [x_i[3 + a : 4 + a] for a in range(3)]
-            n_j = [t_j[at, 3 + a : 4 + a] for a in range(3)]
-            for b, value in enumerate(tile_parts(e, n_i, n_j, soften_sq)):
+            for b, value in enumerate(tile_parts(e, along_col[at], along_row[at], soften_sq)):
                 hi, lo = two_parts(value)
                 tiles[b * 2 * HALF + m * CHUNK : b * 2 * HALF + (m + 1) * CHUNK, :] = hi
                 tiles[b * 2 * HALF + HALF + m * CHUNK : b * 2 * HALF + HALF + (m + 1) * CHUNK, :] = lo
@@ -247,9 +271,15 @@
         got = got[0:8] + got[8:16]
         t = [got[:, b * 2 * HALF : b * 2 * HALF + HALF] + got[:, b * 2 * HALF + HALF : (b + 1) * 2 * HALF] for b in range(3)]
         col_term[k] = jnp.where(first_rows, t[0] - swap(t[2]), swap(t[1]))
+
+    def some_slots(t, carry):
+        for n, tiles in enumerate(tile_bufs):
+            one_slot(t * len(tile_bufs) + n, tiles)
         return carry
 
-    lax.fori_loop(0, used, one_slot, 0)
+    lax.fori_loop(0, used // len(tile_bufs), some_slots, 0)
+    for n in range(used % len(tile_bufs)):
+        one_slot(used - 1 - n, tile_bufs[n])
 
     slot_info = [slot_of(k) for k in range(used)]
     row_ids = [info[0] for info in slot_info]
@@ -383,6 +413,8 @@
             vmem((2, cl_dev, 16, HALF), F32),
             vmem((col_devs * cl_dev, 16, HALF), F32),
             vmem((6 * HALF, PANEL), BF16),
+            vmem((6 * HALF, PANEL), BF16),
+            vmem((6 * HALF, PANEL), BF16),
             vmem((used, 8, PANEL), F32),
             vmem((used, 8, HALF), F32),
             vmem((row_devs, cl_dev, 8, PANEL), F32),

time: 30.6 us -> 27.4 us (0.90)
  Pallas kernels: 28.3 us -> 25.1 us
    pallas_call x1, Pallas kernels: 28.3 us -> 25.1 us  [body(): pl.pallas_call(functools.partial(kernel, sizes), out_shape=jax.ShapeDtype...]
where the time goes in v3:
time: 27.4 us; the launch traced here: 27.1 us
  Pallas kernels  25.1 us (92%)
  local copies, waits for them, and re-layouts  1.38 us (5%)
  between operations  0.66 us (2%)
    pallas_call x1, Pallas kernels, body(): pl.pallas_call(functools.partial(kernel, sizes), out_shape=jax.ShapeDtype...  25.1 us
    unnamed x1, local copies, waits for them, and re-layouts  1.38 us

profile of v3, /device:TPU:0, one launch (start us, length us, event | category | flops | bytes accessed | tf_op | source)
XLA Modules:
  0.0 27.1 jit_solution(16521068193885495823)
XLA Ops:
  0.7 25.1 %shard_map.82 = f32[2,4,1024]{2,1,0:T(4,128)} custom-call(f32[2,4,1024]{2,1,0:T(4,128)} %dens_in.1, f32[3,1024]{1,0:T(4,128)} %pos_in.1, f32[3,1024]{1,0:T(4,128)} %nrm_in.1, f32[1,1024]{1,0:T(1,128)} %bitcast.4, s32[1,1024]{1,0:T(1,128)} %order_in.1, s32[2,12]{1,0:T(2,128)} %pair_in.1, s32[1,12]{1,0:T(1,128)} %bitcast.5, s32[1,1]{1,0:T(1,128)} %bitcast.3.count_in), custom_call_target="tpu_custom_call" | custom-call | tf_op jit(solution)/shard_map/pallas_call | solution.py:393
  25.7 1.4 %copy.11 = f32[2,4,1024]{2,1,0:T(4,128)} copy(f32[2,4,1024]{2,1,0:T(4,128)} %shard_map.82) | data formatting | bytes 65536

commit v4 on v3

--- a/solution.py
+++ b/solution.py
@@ -71,14 +71,16 @@
     dens_in, pos_in, nrm_in, wgt_in, order_in, pair_in, quad_in, count_in,
     out_ref,
     dens_ref, pos_ref, nrm_ref, wgt_ref, order_ref, pair_ref, quad_ref, count_ref, in_sem,
-    onehot, stacked, meta, meta_s, row_buf, col_half, col_buf,
-    tiles_a, tiles_b, tiles_c, row_term, col_term, row_send, col_send, row_recv, col_recv,
+    onehot, stacked, meta, meta_s, row_geo, row_den, col_half, col_geo, col_den,
+    tile_0, tile_1, tile_2, tile_3, tile_4, tile_5, tile_6, tile_7, tile_8, tile_9, row_term, col_term, row_send, col_send, row_recv, col_recv,
     meta_sem, local_sem, row_ssem, row_rsem, col_ssem, col_rsem,
     row_ssem2, row_rsem2, col_ssem2, col_rsem2,
 ):
     n_row, n_col, n_sub, cl_dev, slots, used = sizes
     own = cl_dev * PANEL
-    tile_bufs = (tiles_a, tiles_b, tiles_c)
+    row_buf = (row_geo, row_den)
+    col_buf = (col_geo, col_den)
+    tile_bufs = (tile_0, tile_1, tile_2, tile_3, tile_4, tile_5, tile_6, tile_7, tile_8, tile_9)
     row_devs = n_col * n_sub
     col_devs = n_row * n_sub
     r = lax.axis_index("row")
@@ -134,10 +136,13 @@
     for g in range(cl_dev):
         got = jnp.dot(parts, onehot[:, g * PANEL : (g + 1) * PANEL], preferred_element_type=F32)
         panels = (got[0:16] + got[16:32]) + got[32:48]
-        row_buf[me_row * cl_dev + g] = panels
-        for h in range(2):
-            col_half[h, g] = panels[:, h * HALF : (h + 1) * HALF]
-    col_buf[pl.ds(me_col * cl_dev, cl_dev)] = col_half[s]
+        for kind in range(2):
+            rows = panels[kind * 8 : (kind + 1) * 8]
+            row_buf[kind][me_row * cl_dev + g] = rows
+            for h in range(2):
+                col_half[kind, h, g] = rows[:, h * HALF : (h + 1) * HALF]
+    for kind in range(2):
+        col_buf[kind][pl.ds(me_col * cl_dev, cl_dev)] = col_half[kind, s]
 
     pl.semaphore_wait(barrier, row_devs + col_devs - 2)
 
@@ -148,55 +153,59 @@
     )
     meta_copy.start()
 
-    def col_copy(d):
+    def col_copy(kind, d):
         idx, dev = col_peer(d)
         there = pl.ds(me_col * cl_dev, cl_dev)
         return pltpu.make_async_remote_copy(
-            src_ref=col_half.at[dev["sub"]], dst_ref=col_buf.at[there],
-            send_sem=col_ssem.at[d], recv_sem=col_rsem.at[d],
+            src_ref=col_half.at[kind, dev["sub"]], dst_ref=col_buf[kind].at[there],
+            send_sem=col_ssem.at[kind, d], recv_sem=col_rsem.at[kind, d],
             device_id=dev, device_id_type=MESH,
         )
 
-    def row_copy(d):
+    def row_copy(kind, d):
         idx, dev = row_peer(d)
         here = pl.ds(me_row * cl_dev, cl_dev)
         return pltpu.make_async_remote_copy(
-            src_ref=row_buf.at[here], dst_ref=row_buf.at[here],
-            send_sem=row_ssem.at[d], recv_sem=row_rsem.at[d],
+            src_ref=row_buf[kind].at[here], dst_ref=row_buf[kind].at[here],
+            send_sem=row_ssem.at[kind, d], recv_sem=row_rsem.at[kind, d],
             device_id=dev, device_id_type=MESH,
         )
 
-    def col_arrived(d):
+    def col_arrived(kind, d):
         idx = lax.rem(me_col + col_devs - d, col_devs)
         here = pl.ds(idx * cl_dev, cl_dev)
         pltpu.make_async_remote_copy(
-            src_ref=col_half.at[0], dst_ref=col_buf.at[here],
-            send_sem=col_ssem.at[d], recv_sem=col_rsem.at[d],
+            src_ref=col_half.at[kind, 0], dst_ref=col_buf[kind].at[here],
+            send_sem=col_ssem.at[kind, d], recv_sem=col_rsem.at[kind, d],
             device_id={"sub": other}, device_id_type=MESH,
         ).wait_recv()
 
-    def row_arrived(d):
+    def row_arrived(kind, d):
         idx = lax.rem(me_row + row_devs - d, row_devs)
         here = pl.ds(idx * cl_dev, cl_dev)
         pltpu.make_async_remote_copy(
-            src_ref=row_buf.at[here], dst_ref=row_buf.at[here],
-            send_sem=row_ssem.at[d], recv_sem=row_rsem.at[d],
+            src_ref=row_buf[kind].at[here], dst_ref=row_buf[kind].at[here],
+            send_sem=row_ssem.at[kind, d], recv_sem=row_rsem.at[kind, d],
             device_id={"sub": other}, device_id_type=MESH,
         ).wait_recv()
 
-    for d in range(1, col_devs):
-        col_copy(d).start()
-    for d in range(1, row_devs):
-        row_copy(d).start()
+    def all_arrived(kind):
+        for d in range(1, row_devs):
+            row_arrived(kind, d)
+        for d in range(1, col_devs):
+            col_arrived(kind, d)
+
+    for kind in range(2):
+        for d in range(1, col_devs):
+            col_copy(kind, d).start()
+        for d in range(1, row_devs):
+            row_copy(kind, d).start()
 
     meta_copy.wait()
     to_smem = pltpu.make_async_copy(meta, meta_s, local_sem)
     to_smem.start()
     to_smem.wait()
-    for d in range(1, row_devs):
-        row_arrived(d)
-    for d in range(1, col_devs):
-        col_arrived(d)
+    all_arrived(0)
 
     first_rows = lax.broadcasted_iota(jnp.int32, (8, HALF), 0) < 4
     first_rows_wide = lax.broadcasted_iota(jnp.int32, (8, PANEL), 0) < 4
@@ -228,10 +237,10 @@
     def dot3(a, b):
         return a[0:1] * b[0:1] + a[1:2] * b[1:2] + a[2:3] * b[2:3]
 
-    def one_slot(k, tiles):
+    def make_tile(k, tiles):
         v, u, q = slot_of(k)
-        x_i = row_buf[v]
-        y_j = col_buf[u]
+        x_i = row_geo[v]
+        y_j = col_geo[u]
         q_f = jnp.full((1, PANEL), q, jnp.int32).astype(F32)
         soften_sq = (SOFTEN / q_f) * (SOFTEN / q_f)
         x_in, n_in = x_i[0:3], x_i[3:6]
@@ -242,7 +251,7 @@
         to_row_l = left_parts(jnp.concatenate([-x_jn, one_j, pad_j], axis=0))
         to_col_r = right_parts(jnp.concatenate([x_in, one_i, pad_i], axis=0)).astype(BF16)
         to_row_r = right_parts(jnp.concatenate([n_in, dot3(x_in, n_in), pad_i], axis=0)).astype(BF16)
-        t_j = jnp.transpose(y_j[0:8])
+        t_j = jnp.transpose(y_j)
         along_col = jnp.dot(jnp.transpose(to_col_l).astype(BF16), to_col_r, preferred_element_type=F32)
         along_row = jnp.dot(jnp.transpose(to_row_l).astype(BF16), to_row_r, preferred_element_type=F32)
         for m in range(HALF // CHUNK):
@@ -252,7 +261,10 @@
                 hi, lo = two_parts(value)
                 tiles[b * 2 * HALF + m * CHUNK : b * 2 * HALF + (m + 1) * CHUNK, :] = hi
                 tiles[b * 2 * HALF + HALF + m * CHUNK : b * 2 * HALF + HALF + (m + 1) * CHUNK, :] = lo
-        d_j = y_j[8:16]
+
+    def apply_tile(k, tiles):
+        v, u, _ = slot_of(k)
+        d_j = col_den[u]
         s_j = swap(d_j)
         sig = jnp.where(first_rows, d_j, 0.0)
         mu = jnp.where(first_rows, s_j, 0.0)
@@ -266,20 +278,23 @@
         lhs = jnp.concatenate([sig, sig, mu, mu, adj, adj], axis=1)
         got = jnp.dot(lhs, tiles[...], preferred_element_type=F32)
         row_term[k] = got[0:8] + got[8:16]
-        lhs = stack_parts(x_i[8:16])
+        lhs = stack_parts(row_den[v])
         got = lax.dot_general(lhs, tiles[...], (((1,), (1,)), ((), ())), preferred_element_type=F32)
         got = got[0:8] + got[8:16]
         t = [got[:, b * 2 * HALF : b * 2 * HALF + HALF] + got[:, b * 2 * HALF + HALF : (b + 1) * 2 * HALF] for b in range(3)]
         col_term[k] = jnp.where(first_rows, t[0] - swap(t[2]), swap(t[1]))
 
-    def some_slots(t, carry):
-        for n, tiles in enumerate(tile_bufs):
-            one_slot(t * len(tile_bufs) + n, tiles)
-        return carry
-
-    lax.fori_loop(0, used // len(tile_bufs), some_slots, 0)
-    for n in range(used % len(tile_bufs)):
-        one_slot(used - 1 - n, tile_bufs[n])
+    per_turn = 5
+    turns = [range(t, min(t + per_turn, used)) for t in range(0, used, per_turn)]
+    for n, turn in enumerate(turns):
+        for k in turn:
+            make_tile(k, tile_bufs[k % (2 * per_turn)])
+            if n > 0 and k - per_turn in turns[n - 1]:
+                apply_tile(k - per_turn, tile_bufs[(k - per_turn) % (2 * per_turn)])
+        if n == 0:
+            all_arrived(1)
+    for k in range(used - per_turn, used):
+        apply_tile(k, tile_bufs[k % (2 * per_turn)])
 
     slot_info = [slot_of(k) for k in range(used)]
     row_ids = [info[0] for info in slot_info]
@@ -337,9 +352,11 @@
         row_recv[me_row, g] = row_sum(me_row, g)
 
     for d in range(1, row_devs):
-        row_copy(d).wait_send()
+        row_copy(0, d).wait_send()
+        row_copy(1, d).wait_send()
     for d in range(1, col_devs):
-        col_copy(d).wait_send()
+        col_copy(0, d).wait_send()
+        col_copy(1, d).wait_send()
     for d in range(1, row_devs):
         idx = lax.rem(me_row + row_devs - d, row_devs)
         pltpu.make_async_remote_copy(
@@ -409,12 +426,10 @@
             vmem((16, own), F32),
             vmem((2, 8, 128), jnp.int32),
             pltpu.SMEM((2, 8, 128), jnp.int32),
-            vmem((row_devs * cl_dev, 16, PANEL), F32),
-            vmem((2, cl_dev, 16, HALF), F32),
-            vmem((col_devs * cl_dev, 16, HALF), F32),
-            vmem((6 * HALF, PANEL), BF16),
-            vmem((6 * HALF, PANEL), BF16),
-            vmem((6 * HALF, PANEL), BF16),
+            *[vmem((row_devs * cl_dev, 8, PANEL), F32)] * 2,
+            vmem((2, 2, cl_dev, 8, HALF), F32),
+            *[vmem((col_devs * cl_dev, 8, HALF), F32)] * 2,
+            *[vmem((6 * HALF, PANEL), BF16)] * 10,
             vmem((used, 8, PANEL), F32),
             vmem((used, 8, HALF), F32),
             vmem((row_devs, cl_dev, 8, PANEL), F32),
@@ -423,7 +438,7 @@
             vmem((col_devs, cl_dev, 8, HALF), F32),
             dma((2,)),
             dma,
-            dma((row_devs,)), dma((row_devs,)), dma((col_devs,)), dma((col_devs,)),
+            dma((2, row_devs)), dma((2, row_devs)), dma((2, col_devs)), dma((2, col_devs)),
             dma((row_devs,)), dma((row_devs,)), dma((col_devs,)), dma((col_devs,)),
         ],
         compiler_params=pltpu.CompilerParams(

time: 27.4 us -> 24.7 us (0.901)
  Pallas kernels: 25.1 us -> 22.5 us
    pallas_call x1, Pallas kernels: 25.1 us -> 22.5 us  [body(): pl.pallas_call(functools.partial(kernel, sizes), out_shape=jax.ShapeDtype...]
where the time goes in v4:
time: 24.7 us; the launch traced here: 24.5 us
  Pallas kernels  22.5 us (91%)
  local copies, waits for them, and re-layouts  1.38 us (6%)
  between operations  0.66 us (3%)
    pallas_call x1, Pallas kernels, body(): pl.pallas_call(functools.partial(kernel, sizes), out_shape=jax.ShapeDtype...  22.5 us
    unnamed x1, local copies, waits for them, and re-layouts  1.38 us

profile of v4, /device:TPU:0, one launch (start us, length us, event | category | flops | bytes accessed | tf_op | source)
XLA Modules:
  0.0 24.5 jit_solution(4761606028637079625)
XLA Ops:
  0.7 22.5 %shard_map.82 = f32[2,4,1024]{2,1,0:T(4,128)} custom-call(f32[2,4,1024]{2,1,0:T(4,128)} %dens_in.1, f32[3,1024]{1,0:T(4,128)} %pos_in.1, f32[3,1024]{1,0:T(4,128)} %nrm_in.1, f32[1,1024]{1,0:T(1,128)} %bitcast.4, s32[1,1024]{1,0:T(1,128)} %order_in.1, s32[2,12]{1,0:T(2,128)} %pair_in.1, s32[1,12]{1,0:T(1,128)} %bitcast.5, s32[1,1]{1,0:T(1,128)} %bitcast.3.count_in), custom_call_target="tpu_custom_call" | custom-call | tf_op jit(solution)/shard_map/pallas_call | solution.py:410
  23.1 1.4 %copy.11 = f32[2,4,1024]{2,1,0:T(4,128)} copy(f32[2,4,1024]{2,1,0:T(4,128)} %shard_map.82) | data formatting | bytes 65536
